TPU v7x, 32 devices: a whole 2x2x4 slice. The times are simulated.
32 devices in a mesh: rep: 2 (over y), grp: 4 (over z), loc: 4 (over x, core).
Axes of the slice: x: 2, y: 2, z: 4, core: 2. Of those that a mesh axis runs over, the one named last changes fastest.
Arguments:
- tokens: bfloat16 [4096, 3584], P(('rep', 'grp', 'loc')), parts along dimension 0, may hold values from -6 to 6
- expert_ids: int32 [4096, 8], P(('rep', 'grp', 'loc')), parts along dimension 0, may hold values from 0 to 255, as said below
- route_weights: float32 [4096, 8], P(('rep', 'grp', 'loc')), parts along dimension 0, may hold values from 0.5 to 2.5
- w_gate: bfloat16 [3584, 32768], P(None, ('grp', 'loc')), may hold values from -0.09375 to 0.09375
- w_up: bfloat16 [3584, 32768], P(None, ('grp', 'loc')), may hold values from -0.09375 to 0.09375
- w_down: bfloat16 [3584, 32768], P(None, ('grp', 'loc')), may hold values from -0.1875 to 0.1875
Outputs:
- routed_out: bfloat16 [4096, 3584], P(('rep', 'grp', 'loc')), parts along dimension 0
There are 2 independent parts, one for each index of `rep`. A program takes and returns all parts, laid end to end along the dimension named above; an argument that names none is the same for every part. Nothing has to cross between parts.
Inputs may be any that keep to these rules, and one draw needn't show every extreme that they name: `expert_ids`: each row names 8 different experts, lying in at most 4 of the 8 groups of 32 consecutive ids, and at most one id below 32. In each aligned block of 128 rows (the rows of one device) every id below 32 is named by at most 4 rows, and one such id, the same in every block, by exactly 4.
All inputs are finite; a program needn't handle non-finite values.
Results may differ from a plain program's by a relative error of at most 0.005.
Values may be sent and summed in bfloat16 or wider, within the bound.
A program may use at most 320 MiB of HBM per device.

v0:
```python
import jax
import jax.numpy as jnp
from jax import lax
from jax.sharding import PartitionSpec as P

FF = 1024
EXP_WIN = 32


def send_back(partial_value):
    return lax.all_to_all(partial_value, "grp", split_axis=0, concat_axis=0, tiled=True)


def local(tokens, expert_ids, route_weights, w_gate, w_up, w_down):
    tok_dev, model_width = tokens.shape
    capacity = tok_dev // EXP_WIN
    groups = lax.axis_size("grp")
    loc_ranks = lax.axis_size("loc")
    hid_dev = w_gate.shape[1]
    hid_grp = hid_dev * loc_ranks
    hid_exp = min(FF, hid_grp)
    per_grp = hid_grp // hid_exp
    spread = FF // hid_exp
    slot_count = EXP_WIN * spread * capacity
    flat_ids = expert_ids.reshape(-1)
    flat_weight = route_weights.reshape(-1)
    owner_tok = jnp.arange(flat_ids.shape[0], dtype=jnp.int32) // expert_ids.shape[1]
    inside = flat_ids < EXP_WIN
    onehot = (
        (flat_ids[:, None] == jnp.arange(EXP_WIN, dtype=jnp.int32)[None, :]) & inside[:, None]
    ).astype(jnp.int32)
    before = jnp.cumsum(onehot, 0) - onehot
    rank_in = jnp.sum(before * onehot, 1)
    slot_tok = jnp.full((slot_count + 1,), tok_dev, jnp.int32)
    slot_weight = jnp.zeros((slot_count + 1,), jnp.float32)
    for copy_idx in range(spread):
        where_to = jnp.where(
            inside, (flat_ids * spread + copy_idx) * capacity + rank_in, slot_count
        )
        slot_tok = slot_tok.at[where_to].set(owner_tok)
        slot_weight = slot_weight.at[where_to].set(flat_weight)
    slot_tok = slot_tok[:slot_count]
    slot_weight = slot_weight[:slot_count]
    padded = jnp.concatenate([tokens, jnp.zeros((1, model_width), tokens.dtype)], 0)
    outgoing = padded[slot_tok].reshape(groups, per_grp, capacity, model_width)
    full_down = lax.all_gather(w_down, "loc", axis=1, tiled=True)
    down_cols = full_down.reshape(model_width, per_grp, hid_exp)
    own_exp = max(1, hid_dev // hid_exp)
    own_width = min(hid_dev, hid_exp)
    first_exp = lax.axis_index("loc") * hid_dev // hid_exp
    gate_cols = w_gate.reshape(model_width, own_exp, own_width)
    up_cols = w_up.reshape(model_width, own_exp, own_width)
    everyone = lax.all_gather(
        lax.all_to_all(outgoing, "grp", split_axis=0, concat_axis=0, tiled=True),
        "loc",
        axis=0,
        tiled=True,
    )
    own_rows = lax.dynamic_slice_in_dim(everyone, first_exp, own_exp, 1)
    gate_act = jnp.einsum("njkd,dji->nkji", own_rows, gate_cols, preferred_element_type=jnp.float32)
    up_act = jnp.einsum("njkd,dji->nkji", own_rows, up_cols, preferred_element_type=jnp.float32)
    hidden = (jax.nn.silu(gate_act) * up_act).astype(jnp.bfloat16)
    hidden = hidden.reshape(hidden.shape[0], hidden.shape[1], own_exp * own_width)
    shared = lax.all_to_all(hidden, "loc", split_axis=0, concat_axis=2, tiled=True)
    shared = shared.reshape(shared.shape[0], shared.shape[1], per_grp, hid_exp)
    partial_value = jnp.einsum(
        "skje,dje->sjkd", shared, down_cols, preferred_element_type=jnp.float32
    )
    returned = send_back(partial_value)
    returned = returned.reshape(slot_count, model_width)
    combined = (
        jnp.zeros((tok_dev + 1, model_width), jnp.float32)
        .at[slot_tok]
        .add(returned * slot_weight[:, None])
    )
    return combined[:tok_dev].astype(jnp.bfloat16)


def solution(mesh):
    placed = (
        P(("rep", "grp", "loc"), None),
        P(("rep", "grp", "loc"), None),
        P(("rep", "grp", "loc"), None),
        P(None, ("grp", "loc")),
        P(None, ("grp", "loc")),
        P(None, ("grp", "loc")),
    )
    return jax.shard_map(
        local, mesh=mesh, in_specs=placed, out_specs=P(("rep", "grp", "loc"), None), check_vma=False
    )
```

profile of v0, /device:TPU:0, one launch (start us, length us, event | category | flops | bytes accessed | tf_op | source)
XLA Modules:
  0.0 521.1 jit_solution(14591512145301272386)
XLA Ops:
  6.5 0.7 broadcast_compare_fusion.2
  7.2 0.7 broadcast_multiply_fusion
  7.9 0.8 copy.27
  8.7 0.1 eq.29
  8.8 0.1 eq.25
  8.9 0.1 copy.25
  9.0 0.1 lt.48
  9.1 0.1 copy.26
  9.2 0.1 mul.39
  9.4 9.0 %reduce-window.6 = s32[32,8,128]{2,1,0:T(8,128)S(1)} reduce-window(s32[32,8,128]{2,1,0:T(8,128)S(1)} %fusion.28, s32[]{:T(128)} %constant.50.clone.1), window={size=1x1x128 pad=0_0x0_0x127_0}, to_apply=%region_0.1 | reduce-window | flops 4161536 | bytes 262148 | tf_op jit(solution)/shard_map/reduce-window
  18.4 0.1 slice.23
  18.5 0.1 copy.29
  18.7 0.1 copy.30
  18.7 0.1 broadcast_add_fusion
  18.9 4.3 scatter_custom_fusion
  23.3 1.2 concatenate.3
  24.5 1.1 gather_fusion
  25.6 0.2 reshape.96
  25.8 29.0 %all_to_all.25 = bf16[4,8,4,3584]{3,2,1,0:T(4,128)(2,1)S(1)} all-to-all(bf16[4,8,4,3584]{3,2,1,0:T(4,128)(2,1)S(1)} %reshape.96), channel_id=1, replica_groups=mesh['rep'=2,'grp'=4,'loc'=4] {'grp'}, dimensions={0} | all-to-all | bytes 1835008 | tf_op jit(solution)/shard_map/all_to_all | solution.py:54
  54.9 1.1 copy.31
  55.9 0.0 all-gather.3.cloned.1.call-update
  56.0 0.2 all-gather.5.cloned.1.call-start
  56.2 18.9 %copy.38 = bf16[3584,2048]{0,1:T(8,128)(2,1)} copy(bf16[3584,2048]{1,0:T(8,128)(2,1)} %param.11) | data formatting | bytes 29360128 | tf_op args[5]
  75.1 0.0 all-gather.5.cloned.1.call-update
  75.2 24.9 %reshape.97 = bf16[3584,2,1024]{2,1,0:T(2,128)(2,1)} reshape(bf16[3584,2048]{1,0:T(8,128)(2,1)} %param.9) | data formatting | bytes 29360128 | tf_op jit(solution)/shard_map/reshape | solution.py:51
  100.0 26.4 %reshape.98 = bf16[3584,2,1024]{2,1,0:T(2,128)(2,1)} reshape(bf16[3584,2048]{1,0:T(8,128)(2,1)} %param.10) | data formatting | bytes 29360128 | tf_op jit(solution)/shard_map/reshape | solution.py:52
  126.4 3.5 constant_dynamic-slice_fusion
  129.9 0.0 slice-start.2
  129.9 0.0 slice-start.3
  130.0 10.5 %fusion.6 = f32[16,4,2,1024]{3,0,1,2:T(8,128)S(1)} fusion(bf16[3584,2,1024,1]{2,1,0,3:T(2,128)(2,1)} %bitcast.48, bf16[16,2,4,3584]{3,1,2,0:T(2,128)(2,1)S(1)} %constant_dynamic-slice_fusion), kind=kOutput, calls=%fused_computation.12 | convolution fusion | flops 939524096 | bytes 16121856 | tf_op jit(solution)/shard_map/njkd,dji->nkji/dot_general | solution.py:60
  140.6 6.8 %fusion.15 = bf16[16,4,2,1024]{3,0,1,2:T(8,128)(2,1)S(1)} fusion(bf16[3584,2,1024,1]{2,1,0,3:T(2,128)(2,1)S(1)} %bitcast.47, bf16[16,2,4,3584]{3,1,2,0:T(2,128)(2,1)S(1)} %constant_dynamic-slice_fusion, f32[16,4,2,1024]{3,0,1,2:T(8,128)S(1)} %fusion.6), kind=kOutput, calls=%fused_computation.15 | convolution fusion | flops 940310528 | bytes 16384000 | tf_op jit(solution)/shard_map/njkd,dji->nkji/dot_general | solution.py:61
  147.4 0.3 copy.50
  147.7 0.2 reshape.141
  147.8 11.7 %all_to_all.26 = bf16[16,4,2048]{2,1,0:T(4,128)(2,1)S(1)} all-to-all(bf16[16,4,2048]{2,1,0:T(4,128)(2,1)S(1)} %reshape.141), channel_id=1, replica_groups=mesh['rep'=2,'grp'=4,'loc'=4] {'loc'}, dimensions={0} | all-to-all | bytes 524288 | tf_op jit(solution)/shard_map/all_to_all | solution.py:64
  159.6 0.2 copy.76
  159.8 0.1 reshape.100
  159.8 277.3 %all-gather.5.cloned.1.call-done = bf16[3584,8192]{0,1:T(8,128)(2,1)} async-done(((bf16[3584,2048]{0,1:T(8,128)(2,1)}), bf16[3584,8192]{0,1:T(8,128)(2,1)}) %all-gather.5.cloned.1.call-update) | async-done | bytes 58720272 | tf_op jit(solution)/shard_map/all_gather | solution.py:46
  437.2 20.6 %convolution_bitcast_fusion = f32[4,8,4,3584]{3,2,0,1:T(4,128)S(1)} fusion(bf16[3584,8,1024,1]{0,2,3,1:T(8,128)(2,1)} %bitcast.44, bf16[4,4,8,1024]{3,2,1,0:T(8,128)(2,1)S(1)} %reshape.100), kind=kOutput, calls=%fused_computation.8 | convolution fusion | flops 939524096 | bytes 60817408 | tf_op jit(solution)/shard_map/skje,dje->sjkd/dot_general | solution.py:66
  457.8 0.0 copy-start
  457.8 1.4 copy.41
  459.2 4.6 all-to-all-start.2
  463.8 0.1 copy.42
  463.9 0.1 reshape.124
  464.0 4.3 scatter_custom_fusion.1
  468.3 38.5 %all-to-all-done.2 = f32[4,8,4,3584]{3,2,1,0:T(4,128)S(1)} async-done(((f32[4,8,4,3584]{3,2,1,0:T(4,128)}), f32[4,8,4,3584]{3,2,1,0:T(4,128)S(1)}, u32[]{:S(2)}, u32[]{:S(2)}) %all-to-all-start.2) | async-done | bytes 1835040 | tf_op jit(solution)/shard_map/all_to_all | solution.py:11
  506.8 1.9 reshape.102
  508.7 4.6 scatter_custom_fusion.2
  513.3 1.0 slice.28
  (21 shorter events, 0.2 us)
Async XLA Ops:
  6.5 119.9 %all-gather.3.cloned.1.call-start = ((), (), s32[]{:S(2)}) async-start(), calls=%async_computation.3 | async-start | bytes 4587520 | tf_op jit(solution)/shard_map/all_gather | solution.py:53
  56.0 381.2 %all-gather.5.cloned.1.call-start = ((), (), s32[]{:S(2)}) async-start(), calls=%async_computation.4 | async-start | bytes 73400320 | tf_op jit(solution)/shard_map/all_gather | solution.py:46
  126.4 14.1 %slice-start = ((s8[14680064]{0:T(1024)(128)(4,1)}), s8[4194304]{0:T(1024)(128)(4,1)S(1)}, s32[]{:S(2)}) async-start(s8[14680064]{0:T(1024)(128)(4,1)} %bitcast.45), calls=%async_computation.5 | async-start | bytes 8388608
  129.9 10.6 %slice-start.1 = ((s8[14680064]{0:T(1024)(128)(4,1)}), s8[4194304]{0:T(1024)(128)(4,1)S(1)}, s32[]{:S(2)}) async-start(s8[14680064]{0:T(1024)(128)(4,1)} %bitcast.45), calls=%async_computation.6 | async-start | bytes 8388608
  129.9 10.6 %slice-start.2 = ((s8[14680064]{0:T(1024)(128)(4,1)}), s8[4194304]{0:T(1024)(128)(4,1)S(1)}, s32[]{:S(2)}) async-start(s8[14680064]{0:T(1024)(128)(4,1)} %bitcast.45), calls=%async_computation.7 | async-start | bytes 8388608
  129.9 10.6 %slice-start.3 = ((s8[14680064]{0:T(1024)(128)(4,1)}), s8[2097152]{0:T(1024)(128)(4,1)S(1)}, s32[]{:S(2)}) async-start(s8[14680064]{0:T(1024)(128)(4,1)} %bitcast.45), calls=%async_computation.8 | async-start | bytes 4194304
  457.8 6.0 %copy-start = (f32[128,8]{0,1:T(8,128)S(1)}, f32[128,8]{0,1:T(8,128)}, u32[]{:S(2)}) copy-start(f32[128,8]{0,1:T(8,128)} %param.8) | copy-start | bytes 12292
  459.2 47.6 %all-to-all-start.2 = ((f32[4,8,4,3584]{3,2,1,0:T(4,128)}), f32[4,8,4,3584]{3,2,1,0:T(4,128)S(1)}, u32[]{:S(2)}, u32[]{:S(2)}) async-start(f32[4,8,4,3584]{3,2,1,0:T(4,128)} %copy.41), calls=%async_computation.2 | async-start | bytes 3670016 | tf_op jit(solution)/shard_map/all_to_all | solution.py:11
Sparse Core Ops, SparseCore 0:
  56.1 30.6 all-gather.2
  88.3 348.8 all-gather.4
where the time goes:
time: 523 us; the launch traced here: 521 us
  waiting for transfers between devices  316 us (60%)
  local copies, waits for them, and re-layouts  92.9 us (18%)
  blocking collectives  40.8 us (8%)
  matrix products  38 us (7%)
  other arithmetic  15.2 us (3%)
  between operations  13.7 us (3%)
    all_gather x1, waiting for transfers between devices, local(): full_down = lax.all_gather(w_down, 'loc', axis=1, tiled=True)  277 us
    all_to_all x1, waiting for transfers between devices, send_back(): lax.all_to_all(partial_value, 'grp', split_axis=0, concat_axis=0, tiled=T...  38.5 us
    all_to_all x1, blocking collectives, local(): lax.all_to_all(outgoing, 'grp', split_axis=0, concat_axis=0, tiled=True)  29 us
    reshape x1, local copies, waits for them, and re-layouts, local(): up_cols = w_up.reshape(model_width, own_exp, own_width)  26.4 us
    reshape x1, local copies, waits for them, and re-layouts, local(): gate_cols = w_gate.reshape(model_width, own_exp, own_width)  24.9 us
    dot_general x1, matrix products, local(): jnp.einsum('skje,dje->sjkd', shared, down_cols, preferred_element_type=jn...  20.6 us
    unnamed x13, local copies, waits for them, and re-layouts  19.8 us
    all_to_all x1, blocking collectives, local(): lax.all_to_all(hidden, 'loc', split_axis=0, concat_axis=2, tiled=True)  11.7 us
  transfers between devices with their start and end apart: 3, of which 2 were waited for; matrix products, arithmetic and copies ran while one was open for 18% of the time, Pallas kernels for 0%

commit v1 on v0

--- a/solution.py
+++ b/solution.py
@@ -1,17 +1,276 @@
+import functools
+
 import jax
 import jax.numpy as jnp
 from jax import lax
+from jax.experimental import pallas as pl
+from jax.experimental.pallas import tpu as pltpu
 from jax.sharding import PartitionSpec as P
 
 FF = 1024
 EXP_WIN = 32
+TILE = 16
+MESH = pl.DeviceIdType.MESH
+
+
+def iota(shape, dim):
+    return lax.broadcasted_iota(jnp.int32, shape, dim)
+
+
+def experts_kernel(
+    groups, loc_ranks, own_exp, cap, quarters,
+    ids_ref, weight_ref, tokens_ref, gate_ref, up_ref, down_ref, out_ref,
+    tok, wg, wu, wd, place, send, recv, rows, hidden, stacked, ysend, yrecv, part,
+    tok_sem, w_sem, self_sem, send_sem, recv_sem, yself_sem, ysend_sem, yrecv_sem,
+):
+    devices = groups * loc_ranks
+    tok_dev = tok.shape[0] // quarters
+    quarter = tok.shape[1]
+    slots = devices * cap
+    z, l = lax.axis_index("grp"), lax.axis_index("loc")
+    me = z * loc_ranks + l
+
+    def token_copy(q):
+        return pltpu.make_async_copy(
+            tokens_ref.at[:, pl.ds(q * quarter, quarter)],
+            tok.at[pl.ds(q * tok_dev, tok_dev)],
+            tok_sem.at[q],
+        )
+
+    def weight_copy(m, j):
+        from_ref, to_ref = ((gate_ref, wg), (up_ref, wu), (down_ref, wd))[m]
+        return pltpu.make_async_copy(
+            from_ref.at[:, pl.ds(j * FF, FF)], to_ref.at[j], w_sem.at[m, j]
+        )
+
+    for q in range(quarters):
+        token_copy(q).start()
+    for j in range(own_exp):
+        for m in range(3):
+            weight_copy(m, j).start()
+
+    def each_peer(act):
+        mirror = groups - 1 - z
+        for zz, first in (
+            [(mirror, 0)]
+            + [(lax.rem(mirror + d, groups), 0) for d in range(1, groups)]
+        ):
+            def step(d, carry, zz=zz):
+                ll = lax.rem(l + d, loc_ranks)
+
+                @pl.when(zz * loc_ranks + ll != me)
+                def _():
+                    act(zz, ll, zz * loc_ranks + ll)
+
+                return carry
+
+            lax.fori_loop(first, loc_ranks, step, 0)
+
+    barrier = pltpu.get_barrier_semaphore()
+
+    def greet(zz, ll, peer):
+        pl.semaphore_signal(
+            barrier, inc=1, device_id={"grp": zz, "loc": ll}, device_id_type=MESH
+        )
+
+    each_peer(greet)
+
+    ids = ids_ref[...]
+    inside = ids < EXP_WIN
+    expert = jnp.min(jnp.where(inside, ids, EXP_WIN), 0, keepdims=True)
+    onehot = (iota((EXP_WIN, tok_dev), 0) == expert).astype(jnp.float32)
+    earlier = (iota((tok_dev, tok_dev), 0) < iota((tok_dev, tok_dev), 1)).astype(jnp.bfloat16)
+    before = jnp.dot(onehot.astype(jnp.bfloat16), earlier, preferred_element_type=jnp.float32)
+    rank = jnp.sum(before * onehot, 0, keepdims=True).astype(jnp.int32)
+    weight_row = jnp.sum(jnp.where(inside, weight_ref[...], 0.0), 0, keepdims=True)
+    diagonal = iota((tok_dev, tok_dev), 0) == iota((tok_dev, tok_dev), 1)
+    weight = jnp.sum(jnp.where(diagonal, weight_row, 0.0), 1, keepdims=True)
+    for j in range(own_exp):
+        for q in range(quarters):
+            target = jnp.full_like(expert, -1)
+            for d in range(devices):
+                target = jnp.where(expert == d * own_exp + j, d * TILE + q * cap + rank, target)
+            place[j, :, pl.ds(q * tok_dev, tok_dev)] = (
+                iota((devices * TILE, tok_dev), 0) == target
+            ).astype(jnp.bfloat16)
+    row, col = iota((devices * TILE, devices * TILE), 0), iota((devices * TILE, devices * TILE), 1)
+    home = jnp.zeros_like(row)
+    for q in range(quarters):
+        for d in range(devices):
+            start = q * slots + d * cap
+            home = jnp.where((row >= start) & (row < start + cap), row - start + d * TILE + q * cap, home)
+    spread_out = (col == home).astype(jnp.bfloat16)
+    home = jnp.zeros_like(row)
+    for q in range(quarters):
+        for d in range(devices):
+            start = q * slots + d * cap
+            home = jnp.where((col >= start) & (col < start + cap), col - start + d * TILE + q * cap, home)
+    gather_in = (row == home).astype(jnp.bfloat16)
+
+    for q in range(quarters):
+        token_copy(q).wait()
+
+    def forward(j, zz, ll, peer):
+        return pltpu.make_async_remote_copy(
+            src_ref=send.at[j, peer], dst_ref=recv.at[j, me],
+            send_sem=send_sem.at[j, peer], recv_sem=recv_sem.at[j, me],
+            device_id={"grp": zz, "loc": ll}, device_id_type=MESH,
+        )
+
+    def arrived(j, zz, ll, peer):
+        return pltpu.make_async_remote_copy(
+            src_ref=send.at[j, peer], dst_ref=recv.at[j, peer],
+            send_sem=send_sem.at[j, peer], recv_sem=recv_sem.at[j, peer],
+            device_id={"grp": zz, "loc": ll}, device_id_type=MESH,
+        )
+
+    def back(j, zz, ll, peer):
+        return pltpu.make_async_remote_copy(
+            src_ref=ysend.at[j, peer], dst_ref=yrecv.at[j, me],
+            send_sem=ysend_sem.at[j, peer], recv_sem=yrecv_sem.at[j, me],
+            device_id={"grp": zz, "loc": ll}, device_id_type=MESH,
+        )
+
+    def returned(j, zz, ll, peer):
+        return pltpu.make_async_remote_copy(
+            src_ref=ysend.at[j, peer], dst_ref=yrecv.at[j, peer],
+            send_sem=ysend_sem.at[j, peer], recv_sem=yrecv_sem.at[j, peer],
+            device_id={"grp": zz, "loc": ll}, device_id_type=MESH,
+        )
+
+    def own_forward(j):
+        return pltpu.make_async_copy(send.at[j, me], recv.at[j, me], self_sem.at[j])
+
+    def own_back(j):
+        return pltpu.make_async_copy(ysend.at[j, me], yrecv.at[j, me], yself_sem.at[j])
+
+    for j in range(own_exp):
+        picked = jnp.dot(place[j], tok[...], preferred_element_type=jnp.float32)
+        send[j] = picked.astype(jnp.bfloat16).reshape(devices, TILE, quarter)
+        if j == 0:
+            pl.semaphore_wait(barrier, devices - 1)
+        each_peer(lambda zz, ll, peer: forward(j, zz, ll, peer).start())
+        own_forward(j).start()
+
+    step = 256
+    for j in range(own_exp):
+        each_peer(lambda zz, ll, peer: arrived(j, zz, ll, peer).wait_recv())
+        own_forward(j).wait()
+        ordered = jnp.dot(
+            spread_out, recv[j].reshape(devices * TILE, quarter),
+            preferred_element_type=jnp.float32,
+        ).astype(jnp.bfloat16)
+        for q in range(quarters):
+            rows[:, pl.ds(q * quarter, quarter)] = ordered[q * slots : (q + 1) * slots]
+        weight_copy(0, j).wait()
+        weight_copy(1, j).wait()
+
+        def gate_up(n, carry):
+            at = pl.ds(pl.multiple_of(n * step, step), step)
+            gate = jnp.dot(rows[...], wg[j, :, at], preferred_element_type=jnp.float32)
+            up = jnp.dot(rows[...], wu[j, :, at], preferred_element_type=jnp.float32)
+            hidden[:, at] = (gate / (1.0 + jnp.exp(-gate)) * up).astype(jnp.bfloat16)
+            return carry
+
+        lax.fori_loop(0, FF // step, gate_up, 0)
+        weight_copy(2, j).wait()
+
+        def down(q, carry):
+            product = lax.dot_general(
+                hidden[...], wd[j, pl.ds(pl.multiple_of(q * quarter, quarter), quarter), :],
+                (((1,), (1,)), ((), ())), preferred_element_type=jnp.float32,
+            )
+            stacked[pl.ds(pl.multiple_of(q * slots, slots), slots), :] = product.astype(jnp.bfloat16)
+            return carry
+
+        lax.fori_loop(0, quarters, down, 0)
+        ysend[j] = (
+            jnp.dot(gather_in, stacked[...], preferred_element_type=jnp.float32)
+            .astype(jnp.bfloat16)
+            .reshape(devices, TILE, quarter)
+        )
+        each_peer(lambda zz, ll, peer: back(j, zz, ll, peer).start())
+        own_back(j).start()
+
+    for j in range(own_exp):
+        each_peer(lambda zz, ll, peer: returned(j, zz, ll, peer).wait_recv())
+        own_back(j).wait()
+        blocks = yrecv[j].reshape(devices * TILE, quarter)
+        for q in range(quarters):
+            at = pl.ds(q * quarter, quarter)
+            chosen = lax.dot_general(
+                place[j, :, pl.ds(q * tok_dev, tok_dev)], blocks,
+                (((0,), (0,)), ((), ())), preferred_element_type=jnp.float32,
+            )
+            if j > 0:
+                chosen = chosen + part[:, at].astype(jnp.float32)
+            if j < own_exp - 1:
+                part[:, at] = chosen.astype(jnp.bfloat16)
+            else:
+                out_ref[:, at] = (chosen * weight).astype(jnp.bfloat16)
+
+    for j in range(own_exp):
+        each_peer(lambda zz, ll, peer: forward(j, zz, ll, peer).wait_send())
+        each_peer(lambda zz, ll, peer: back(j, zz, ll, peer).wait_send())
+
+
+def whole_experts(tokens, expert_ids, route_weights, w_gate, w_up, w_down):
+    tok_dev, width = tokens.shape
+    cap = tok_dev // EXP_WIN
+    groups, loc_ranks = lax.axis_size("grp"), lax.axis_size("loc")
+    devices = groups * loc_ranks
+    own_exp = w_gate.shape[1] // FF
+    quarters = TILE // cap
+    quarter = width // quarters
+    slots = devices * cap
+    bf16 = jnp.bfloat16
+    anywhere, vmem = pl.BlockSpec(memory_space=pl.ANY), pl.BlockSpec(memory_space=pltpu.VMEM)
+    dma = pltpu.SemaphoreType.DMA
+    block = pltpu.VMEM((own_exp, devices, TILE, quarter), bf16)
+    return pl.pallas_call(
+        functools.partial(experts_kernel, groups, loc_ranks, own_exp, cap, quarters),
+        out_shape=jax.ShapeDtypeStruct((tok_dev, width), bf16),
+        in_specs=[vmem, vmem, anywhere, anywhere, anywhere, anywhere],
+        out_specs=vmem,
+        scratch_shapes=[
+            pltpu.VMEM((quarters * tok_dev, quarter), bf16),
+            pltpu.VMEM((own_exp, width, FF), bf16),
+            pltpu.VMEM((own_exp, width, FF), bf16),
+            pltpu.VMEM((own_exp, width, FF), bf16),
+            pltpu.VMEM((own_exp, devices * TILE, quarters * tok_dev), bf16),
+            block,
+            block,
+            pltpu.VMEM((slots, width), bf16),
+            pltpu.VMEM((slots, FF), bf16),
+            pltpu.VMEM((quarters * slots, quarter), bf16),
+            block,
+            block,
+            pltpu.VMEM((tok_dev, width), bf16),
+            dma((quarters,)),
+            dma((3, own_exp)),
+            dma((own_exp,)),
+            dma((own_exp, devices)),
+            dma((own_exp, devices)),
+            dma((own_exp,)),
+            dma((own_exp, devices)),
+            dma((own_exp, devices)),
+        ],
+        compiler_params=pltpu.CompilerParams(
+            collective_id=0, has_side_effects=True, vmem_limit_bytes=60 * 2**20
+        ),
+        cost_estimate=pl.CostEstimate(
+            flops=6 * slots * own_exp * width * FF,
+            bytes_accessed=6 * own_exp * width * FF,
+            transcendentals=slots * own_exp * FF,
+        ),
+    )(expert_ids.T, route_weights.T, tokens, w_gate, w_up, w_down)
 
 
 def send_back(partial_value):
     return lax.all_to_all(partial_value, "grp", split_axis=0, concat_axis=0, tiled=True)
 
 
-def local(tokens, expert_ids, route_weights, w_gate, w_up, w_down):
+def split_experts(tokens, expert_ids, route_weights, w_gate, w_up, w_down):
     tok_dev, model_width = tokens.shape
     capacity = tok_dev // EXP_WIN
     groups = lax.axis_size("grp")
@@ -76,6 +335,22 @@
     return combined[:tok_dev].astype(jnp.bfloat16)
 
 
+def local(tokens, expert_ids, route_weights, w_gate, w_up, w_down):
+    tok_dev, width = tokens.shape
+    devices = lax.axis_size("grp") * lax.axis_size("loc")
+    cap = tok_dev // EXP_WIN
+    whole = (
+        w_gate.shape[1] % FF == 0
+        and devices * w_gate.shape[1] == EXP_WIN * FF
+        and tok_dev % EXP_WIN == 0
+        and tok_dev % 128 == 0
+        and TILE % cap == 0
+        and width % (128 * (TILE // cap)) == 0
+    )
+    plan = whole_experts if whole else split_experts
+    return plan(tokens, expert_ids, route_weights, w_gate, w_up, w_down)
+
+
 def solution(mesh):
     placed = (
         P(("rep", "grp", "loc"), None),

time: 523 us -> 63.1 us (0.12)
  waiting for transfers between devices: 316 us -> 0 us
  local copies, waits for them, and re-layouts: 92.9 us -> 2.16 us
  Pallas kernels: 0 us -> 60.8 us
  blocking collectives: 40.8 us -> 0 us
  matrix products: 38 us -> 0 us
  other arithmetic: 15.2 us -> 0 us
  between operations: 13.7 us -> 0.01 us
    all_gather x2 -> x0, waiting for transfers between devices: 277 us -> none  [the longest x1 277 us: local(): full_down = lax.all_gather(w_down, 'loc', axis=1, tiled=True)]
    pallas_call x0 -> x1, Pallas kernels: none -> 60.8 us  [whole_experts(): pl.pallas_call(functools.partial(experts_kernel, groups, loc_ranks, own_e...]
    reshape x8 -> x0, local copies, waits for them, and re-layouts: 53.9 us -> none  [the longest x1 26.4 us: local(): up_cols = w_up.reshape(model_width, own_exp, own_width)]
    all_to_all x2 -> x0, blocking collectives: 40.8 us -> none  [the longest x1 29 us: local(): lax.all_to_all(outgoing, 'grp', split_axis=0, concat_axis=0, tiled=True)]
    all_to_all x1 -> x0, waiting for transfers between devices: 38.5 us -> none  [send_back(): lax.all_to_all(partial_value, 'grp', split_axis=0, concat_axis=0, tiled=T...]
    dot_general x3 -> x0, matrix products: 38 us -> none  [the longest x1 20.6 us: local(): jnp.einsum('skje,dje->sjkd', shared, down_cols, preferred_element_type=jn...]
    unnamed x13 -> x1, local copies, waits for them, and re-layouts: 19.8 us -> 2.16 us
    another operation x3 -> x0, other arithmetic: 9.15 us -> none
  transfers between devices with their start and end apart: 3 -> 0, of which waited for: 2 -> 0; matrix products, arithmetic and copies ran while one was open for 18% -> 0% of each run, Pallas kernels for 0% -> 0%
where the time goes in v1:
time: 63.1 us; the launch traced here: 62.9 us
  Pallas kernels  60.8 us (96%)
  local copies, waits for them, and re-layouts  2.16 us (3%)
    pallas_call x1, Pallas kernels, whole_experts(): pl.pallas_call(functools.partial(experts_kernel, groups, loc_ranks, own_e...  60.8 us
    unnamed x1, local copies, waits for them, and re-layouts  2.16 us

profile of v1, /device:TPU:0, one launch (start us, length us, event | category | flops | bytes accessed | tf_op | source)
XLA Modules:
  0.0 62.9 jit_solution(995616375245775763)
XLA Ops:
  0.0 60.8 %shard_map.64 = bf16[128,3584]{1,0:T(8,128)(2,1)} custom-call(s32[8,128]{1,0:T(8,128)} %bitcast.2, f32[8,128]{1,0:T(8,128)} %bitcast.3, bf16[128,3584]{1,0:T(8,128)(2,1)} %tokens_ref.1, bf16[3584,2048]{1,0:T(8,128)(2,1)} %gate_ref.1, bf16[3584,2048]{1,0:T(8,128)(2,1)} %up_ref.1, bf16[3584,2048]{1,0:T(8,128)(2,1)} %down_ref.1), custom_call_target="tpu_custom_call" | custom-call | flops 2818572288 | bytes 44040192 | tf_op jit(solution)/shard_map/pallas_call | solution.py:230
  60.8 2.2 %copy.8 = bf16[128,3584]{1,0:T(8,128)(2,1)} copy(bf16[128,3584]{1,0:T(8,128)(2,1)} %shard_map.64) | data formatting | bytes 1835008

commit v2 on v1

--- a/solution.py
+++ b/solution.py
@@ -15,6 +15,10 @@
 
 def iota(shape, dim):
     return lax.broadcasted_iota(jnp.int32, shape, dim)
+
+
+def quotient(values, power_of_two):
+    return lax.shift_right_logical(values, power_of_two.bit_length() - 1)
 
 
 def experts_kernel(
@@ -45,10 +49,6 @@
 
     for q in range(quarters):
         token_copy(q).start()
-    for j in range(own_exp):
-        for m in range(3):
-            weight_copy(m, j).start()
-
     def each_peer(act):
         mirror = groups - 1 - z
         for zz, first in (
@@ -87,25 +87,14 @@
     weight = jnp.sum(jnp.where(diagonal, weight_row, 0.0), 1, keepdims=True)
     for j in range(own_exp):
         for q in range(quarters):
-            target = jnp.full_like(expert, -1)
-            for d in range(devices):
-                target = jnp.where(expert == d * own_exp + j, d * TILE + q * cap + rank, target)
+            target = jnp.where(
+                (expert & (own_exp - 1)) == j,
+                quotient(expert, own_exp) * TILE + q * cap + rank,
+                -1,
+            )
             place[j, :, pl.ds(q * tok_dev, tok_dev)] = (
                 iota((devices * TILE, tok_dev), 0) == target
             ).astype(jnp.bfloat16)
-    row, col = iota((devices * TILE, devices * TILE), 0), iota((devices * TILE, devices * TILE), 1)
-    home = jnp.zeros_like(row)
-    for q in range(quarters):
-        for d in range(devices):
-            start = q * slots + d * cap
-            home = jnp.where((row >= start) & (row < start + cap), row - start + d * TILE + q * cap, home)
-    spread_out = (col == home).astype(jnp.bfloat16)
-    home = jnp.zeros_like(row)
-    for q in range(quarters):
-        for d in range(devices):
-            start = q * slots + d * cap
-            home = jnp.where((col >= start) & (col < start + cap), col - start + d * TILE + q * cap, home)
-    gather_in = (row == home).astype(jnp.bfloat16)
 
     for q in range(quarters):
         token_copy(q).wait()
@@ -151,6 +140,14 @@
             pl.semaphore_wait(barrier, devices - 1)
         each_peer(lambda zz, ll, peer: forward(j, zz, ll, peer).start())
         own_forward(j).start()
+        for m in range(3):
+            weight_copy(m, j).start()
+
+    col = iota((1, devices * TILE), 1)
+    home = quotient(col & (slots - 1), cap) * TILE + quotient(col, slots) * cap + (col & (cap - 1))
+    gather_in = (iota((devices * TILE, devices * TILE), 0) == home).astype(jnp.bfloat16)
+    home = quotient(col & (TILE - 1), cap) * slots + quotient(col, TILE) * cap + (col & (cap - 1))
+    spread_out = (iota((devices * TILE, devices * TILE), 0) == home).astype(jnp.bfloat16)
 
     step = 256
     for j in range(own_exp):
@@ -345,6 +342,7 @@
         and tok_dev % EXP_WIN == 0
         and tok_dev % 128 == 0
         and TILE % cap == 0
+        and devices & (devices - 1) == 0
         and width % (128 * (TILE // cap)) == 0
     )
     plan = whole_experts if whole else split_experts

time: 63.1 us -> 53.2 us (0.84)
  Pallas kernels: 60.8 us -> 50.8 us
    pallas_call x1, Pallas kernels: 60.8 us -> 50.8 us  [whole_experts(): pl.pallas_call(functools.partial(experts_kernel, groups, loc_ranks, own_e...]
where the time goes in v2:
time: 53.2 us; the launch traced here: 53 us
  Pallas kernels  50.8 us (95%)
  local copies, waits for them, and re-layouts  2.16 us (4%)
    pallas_call x1, Pallas kernels, whole_experts(): pl.pallas_call(functools.partial(experts_kernel, groups, loc_ranks, own_e...  50.8 us
    unnamed x1, local copies, waits for them, and re-layouts  2.16 us

profile of v2, /device:TPU:0, one launch (start us, length us, event | category | flops | bytes accessed | tf_op | source)
XLA Modules:
  0.0 53.0 jit_solution(12852484360391355003)
XLA Ops:
  0.0 50.8 %shard_map.64 = bf16[128,3584]{1,0:T(8,128)(2,1)} custom-call(s32[8,128]{1,0:T(8,128)} %bitcast.2, f32[8,128]{1,0:T(8,128)} %bitcast.3, bf16[128,3584]{1,0:T(8,128)(2,1)} %tokens_ref.1, bf16[3584,2048]{1,0:T(8,128)(2,1)} %gate_ref.1, bf16[3584,2048]{1,0:T(8,128)(2,1)} %up_ref.1, bf16[3584,2048]{1,0:T(8,128)(2,1)} %down_ref.1), custom_call_target="tpu_custom_call" | custom-call | flops 2818572288 | bytes 44040192 | tf_op jit(solution)/shard_map/pallas_call | solution.py:227
  50.8 2.2 %copy.8 = bf16[128,3584]{1,0:T(8,128)(2,1)} copy(bf16[128,3584]{1,0:T(8,128)(2,1)} %shard_map.64) | data formatting | bytes 1835008
